TPU v7x, 32 devices: a whole 2x2x4 slice. The times are simulated.
32 devices in a mesh: fsdp: 4 (over y, x), ctx: 8 (over z, core).
Axes of the slice: x: 2, y: 2, z: 4, core: 2. Of those that a mesh axis runs over, the one named last changes fastest.
Arguments:
- x_in: bfloat16 [8, 2048, 960], P('fsdp', 'ctx'), may hold values from -6 to 6
- positions: int32 [8, 2048], P('fsdp'), may hold values from 0 to 2047, as said below
- norm_one: bfloat16 [960], P('fsdp'), may hold values from 0.099609375 to 1.8984375
- w_query: bfloat16 [960, 960], P('fsdp'), may hold values from -0.1875 to 0.1875
- w_key: bfloat16 [960, 320], P('fsdp'), may hold values from -0.1875 to 0.1875
- w_value: bfloat16 [960, 320], P('fsdp'), may hold values from -0.1875 to 0.1875
- w_output: bfloat16 [960, 960], P('fsdp'), may hold values from -6 to 6
- norm_two: bfloat16 [960], P('fsdp'), may hold values from 0.099609375 to 1.8984375
- w_gate: bfloat16 [960, 2560], P('fsdp'), may hold values from -0.1875 to 0.1875
- w_up: bfloat16 [960, 2560], P('fsdp'), may hold values from -0.1875 to 0.1875
- w_down: bfloat16 [2560, 960], P('fsdp'), may hold values from -0.125 to 0.125
- cotangent: bfloat16 [8, 2048, 960], P('fsdp', 'ctx'), may hold values from -6 to 6
Outputs:
- out: bfloat16 [8, 2048, 960], P('fsdp', 'ctx')
- grad_in: bfloat16 [8, 2048, 960], P('fsdp', 'ctx')
- grad_norm_one: float32 [960], P('fsdp')
- grad_w_query: float32 [960, 960], P('fsdp')
- grad_w_key: float32 [960, 320], P('fsdp')
- grad_w_value: float32 [960, 320], P('fsdp')
- grad_w_output: float32 [960, 960], P('fsdp')
- grad_norm_two: float32 [960], P('fsdp')
- grad_w_gate: float32 [960, 2560], P('fsdp')
- grad_w_up: float32 [960, 2560], P('fsdp')
- grad_w_down: float32 [2560, 960], P('fsdp')
Inputs may be any that keep to these rules, and one draw needn't show every extreme that they name: In each sequence the rows form aligned blocks of 256; the rows of a block hold 256 consecutive positions in order, and the blocks' first positions are the multiples of 256 below 2048 in some order, each once.
All inputs are finite; a program needn't handle non-finite values.
Results may differ from a plain program's by a relative error of at most 0.02.
Values may be sent and summed in bfloat16 or wider, within the bound.
A program may use at most 192 MiB of HBM per device.

v0:
```python
import math

import jax
import jax.numpy as jnp
from jax import lax
from jax.sharding import PartitionSpec as P

HEADS = 15
KV_HEADS = 5
HEAD = 64


epsilon = 1e-05
rope_log_base = math.log(100000.0)
masked_value = -1e30


def matmul(left, right):
    return jnp.dot(left, right, preferred_element_type=jnp.float32)


def left_transposed(left, right):
    return lax.dot_general(
        left, right, (((0,), (0,)), ((), ())), preferred_element_type=jnp.float32
    )


def right_transposed(left, right):
    return lax.dot_general(
        left, right, (((1,), (1,)), ((), ())), preferred_element_type=jnp.float32
    )


def angle_tables(places):
    half = HEAD // 2
    freqs = jnp.exp(-rope_log_base * (2.0 * jnp.arange(half, dtype=jnp.float32) / HEAD))
    angles = places.astype(jnp.float32)[:, None, None] * freqs[None, None, :]
    return (jnp.cos(angles), jnp.sin(angles))


def rotate(values, cosine, sine):
    half = values.shape[-1] // 2
    first = values[..., :half]
    second = values[..., half:]
    return jnp.concatenate(
        [first * cosine - second * sine, second * cosine + first * sine], axis=-1
    )


def unrotate(grads, cosine, sine):
    half = grads.shape[-1] // 2
    first = grads[..., :half]
    second = grads[..., half:]
    return jnp.concatenate(
        [first * cosine + second * sine, second * cosine - first * sine], axis=-1
    )


def norm_forward(values, gain):
    inverse_scale = lax.rsqrt(jnp.mean(values * values, axis=1, keepdims=True) + epsilon)
    return (values * inverse_scale * gain, inverse_scale)


def norm_backward(values, inverse_scale, gain, upstream):
    scaled = gain * upstream
    inner = jnp.mean(scaled * values, axis=1, keepdims=True)
    grad_values = (
        inverse_scale * scaled - values * (inverse_scale * inverse_scale * inverse_scale) * inner
    )
    grad_gain = jnp.sum(upstream * values * inverse_scale, axis=0)
    return (grad_values, grad_gain)


def block_scores(query, query_places, key_block, place_block, scale):
    logits = (
        jnp.einsum("rgah,kgh->gark", query, key_block, preferred_element_type=jnp.float32) * scale
    )
    allowed = place_block[None, None, None, :] <= query_places[None, None, :, None]
    return (logits, allowed)


def split_blocks(keys, values, key_places):
    length = keys.shape[0]
    block = min(512, length)
    count = length // block
    key_blocks = keys.reshape(count, block, keys.shape[1], keys.shape[2])
    value_blocks = values.reshape(count, block, values.shape[1], values.shape[2])
    place_blocks = key_places.reshape(count, block)
    return (key_blocks, value_blocks, place_blocks)


def attend_forward(query, query_places, keys, values, key_places):
    scale = 1.0 / math.sqrt(HEAD)
    key_blocks, value_blocks, place_blocks = split_blocks(keys, values, key_places)
    stat_shape = (query.shape[1], query.shape[2], query.shape[0])

    def gather_stats(carry, element):
        running_peak, running_total = carry
        key_block, place_block = element
        logits, allowed = block_scores(query, query_places, key_block, place_block, scale)
        new_peak = jnp.maximum(
            running_peak, jnp.max(jnp.where(allowed, logits, masked_value), axis=3)
        )
        terms = jnp.exp(jnp.where(allowed, logits - new_peak[..., None], masked_value))
        new_total = running_total * jnp.exp(running_peak - new_peak) + jnp.sum(terms, axis=3)
        return ((new_peak, new_total), None)

    start = (jnp.full(stat_shape, masked_value, jnp.float32), jnp.zeros(stat_shape, jnp.float32))
    (peak, total), unused = lax.scan(gather_stats, start, (key_blocks, place_blocks))
    shift = peak + jnp.log(total)

    def weigh(carry, element):
        key_block, value_block, place_block = element
        logits, allowed = block_scores(query, query_places, key_block, place_block, scale)
        weights = jnp.exp(jnp.where(allowed, logits - shift[..., None], masked_value)).astype(
            jnp.bfloat16
        )
        return (
            carry
            + jnp.einsum(
                "gark,kgh->rgah", weights, value_block, preferred_element_type=jnp.float32
            ),
            None,
        )

    result, unused = lax.scan(
        weigh, jnp.zeros(query.shape, jnp.float32), (key_blocks, value_blocks, place_blocks)
    )
    return (result, shift)


def attend_backward(query, query_places, keys, values, key_places, shift, upstream, output):
    scale = 1.0 / math.sqrt(HEAD)
    key_blocks, value_blocks, place_blocks = split_blocks(keys, values, key_places)
    delta = jnp.einsum("rgah,rgah->gar", upstream.astype(jnp.float32), output)

    def accumulate(carry, element):
        key_block, value_block, place_block = element
        logits, allowed = block_scores(query, query_places, key_block, place_block, scale)
        weights = jnp.exp(jnp.where(allowed, logits - shift[..., None], masked_value))
        rounded = weights.astype(jnp.bfloat16)
        grad_weights = jnp.einsum(
            "rgah,kgh->gark", upstream, value_block, preferred_element_type=jnp.float32
        )
        grad_logits = (weights * (grad_weights - delta[..., None])).astype(jnp.bfloat16)
        carry = (
            carry
            + jnp.einsum(
                "gark,kgh->rgah", grad_logits, key_block, preferred_element_type=jnp.float32
            )
            * scale
        )
        grad_key = (
            jnp.einsum("gark,rgah->kgh", grad_logits, query, preferred_element_type=jnp.float32)
            * scale
        )
        grad_value = jnp.einsum(
            "gark,rgah->kgh", rounded, upstream, preferred_element_type=jnp.float32
        )
        return (carry, (grad_key, grad_value))

    grad_query, stacked = lax.scan(
        accumulate, jnp.zeros(query.shape, jnp.float32), (key_blocks, value_blocks, place_blocks)
    )
    return (grad_query, stacked[0].reshape(keys.shape), stacked[1].reshape(values.shape))


def on_device(
    x_in,
    positions,
    norm_one,
    w_query,
    w_key,
    w_value,
    w_output,
    norm_two,
    w_gate,
    w_up,
    w_down,
    cotangent,
):
    seqs, rows, width = x_in.shape
    total_rows = seqs * rows
    groups = HEADS // KV_HEADS
    kv_width = KV_HEADS * HEAD
    gain_one, query_w, key_w, value_w, output_w = (
        lax.all_gather(norm_one, "fsdp", axis=0, tiled=True),
        lax.all_gather(w_query, "fsdp", axis=0, tiled=True),
        lax.all_gather(w_key, "fsdp", axis=0, tiled=True),
        lax.all_gather(w_value, "fsdp", axis=0, tiled=True),
        lax.all_gather(w_output, "fsdp", axis=0, tiled=True),
    )
    gain_two, gate_w, up_w, down_w = (
        lax.all_gather(norm_two, "fsdp", axis=0, tiled=True),
        lax.all_gather(w_gate, "fsdp", axis=0, tiled=True),
        lax.all_gather(w_up, "fsdp", axis=0, tiled=True),
        lax.all_gather(w_down, "fsdp", axis=0, tiled=True),
    )
    own_places = lax.dynamic_slice_in_dim(positions, lax.axis_index("ctx") * rows, rows, 1)
    cosine, sine = angle_tables(own_places.reshape(total_rows))
    inputs = x_in.reshape(total_rows, width).astype(jnp.float32)
    first_gain = gain_one.astype(jnp.float32)
    normed, first_scale = norm_forward(inputs, first_gain)
    normed_one = normed.astype(jnp.bfloat16)
    query = rotate(
        matmul(normed_one, query_w).reshape(total_rows, HEADS, HEAD), cosine, sine
    ).astype(jnp.bfloat16)
    own_keys = rotate(matmul(normed_one, key_w).reshape(total_rows, KV_HEADS, HEAD), cosine, sine)
    own_keys = own_keys.astype(jnp.bfloat16).reshape(seqs, rows, kv_width)
    own_values = matmul(normed_one, value_w).astype(jnp.bfloat16).reshape(seqs, rows, kv_width)
    all_keys, all_values = (
        lax.all_gather(own_keys, "ctx", axis=1, tiled=True),
        lax.all_gather(own_values, "ctx", axis=1, tiled=True),
    )
    length = all_keys.shape[1]
    grouped_query = query.reshape(seqs, rows, KV_HEADS, groups, HEAD)
    key_heads = all_keys.reshape(seqs, length, KV_HEADS, HEAD)
    value_heads = all_values.reshape(seqs, length, KV_HEADS, HEAD)
    attended, shift = jax.vmap(attend_forward)(
        grouped_query, own_places, key_heads, value_heads, positions
    )
    attended_low = attended.astype(jnp.bfloat16).reshape(total_rows, HEADS * HEAD)
    hidden = inputs + matmul(attended_low, output_w)
    second_gain = gain_two.astype(jnp.float32)
    normed, second_scale = norm_forward(hidden, second_gain)
    normed_two = normed.astype(jnp.bfloat16)
    gate = matmul(normed_two, gate_w)
    upper = matmul(normed_two, up_w)
    sigmoid = jax.nn.sigmoid(gate)
    activated = (gate * sigmoid * upper).astype(jnp.bfloat16)
    output = hidden + matmul(activated, down_w)
    upstream = cotangent.reshape(total_rows, width)
    grad_act = right_transposed(upstream, down_w)
    grad_gate = (grad_act * upper * sigmoid * (1.0 + gate * (1.0 - sigmoid))).astype(jnp.bfloat16)
    grad_upper = (grad_act * gate * sigmoid).astype(jnp.bfloat16)
    grad_normed_two = right_transposed(grad_gate, gate_w) + right_transposed(grad_upper, up_w)
    grad_hidden, grad_gain_two = norm_backward(hidden, second_scale, second_gain, grad_normed_two)
    grad_hidden = grad_hidden + upstream.astype(jnp.float32)
    grad_branch = grad_hidden.astype(jnp.bfloat16)
    grad_attended = right_transposed(grad_branch, output_w).astype(jnp.bfloat16)
    grad_attended = grad_attended.reshape(seqs, rows, KV_HEADS, groups, HEAD)
    grad_query, grad_keys, grad_values = jax.vmap(attend_backward)(
        grouped_query, own_places, key_heads, value_heads, positions, shift, grad_attended, attended
    )
    own_grad_keys, own_grad_values = (
        lax.psum_scatter(
            grad_keys.reshape(seqs, length, kv_width).astype(jnp.bfloat16),
            "ctx",
            scatter_dimension=1,
            tiled=True,
        ).astype(jnp.float32),
        lax.psum_scatter(
            grad_values.reshape(seqs, length, kv_width).astype(jnp.bfloat16),
            "ctx",
            scatter_dimension=1,
            tiled=True,
        ).astype(jnp.float32),
    )
    grad_query_low = unrotate(grad_query.reshape(total_rows, HEADS, HEAD), cosine, sine)
    grad_query_low = grad_query_low.astype(jnp.bfloat16).reshape(total_rows, HEADS * HEAD)
    grad_key_low = unrotate(own_grad_keys.reshape(total_rows, KV_HEADS, HEAD), cosine, sine)
    grad_key_low = grad_key_low.astype(jnp.bfloat16).reshape(total_rows, kv_width)
    grad_value_low = own_grad_values.reshape(total_rows, kv_width).astype(jnp.bfloat16)
    grad_normed_one = (
        right_transposed(grad_query_low, query_w)
        + right_transposed(grad_key_low, key_w)
        + right_transposed(grad_value_low, value_w)
    )
    grad_inputs, grad_gain_one = norm_backward(inputs, first_scale, first_gain, grad_normed_one)
    grad_inputs = grad_inputs + grad_hidden
    result_out = output.astype(jnp.bfloat16).reshape(seqs, rows, width)
    result_grad = grad_inputs.astype(jnp.bfloat16).reshape(seqs, rows, width)
    right_all = (
        lax.all_gather(grad_query_low, "fsdp", axis=0, tiled=True),
        lax.all_gather(grad_key_low, "fsdp", axis=0, tiled=True),
        lax.all_gather(grad_value_low, "fsdp", axis=0, tiled=True),
        lax.all_gather(grad_branch, "fsdp", axis=0, tiled=True),
        lax.all_gather(grad_gate, "fsdp", axis=0, tiled=True),
        lax.all_gather(grad_upper, "fsdp", axis=0, tiled=True),
        lax.all_gather(upstream, "fsdp", axis=0, tiled=True),
    )
    left_all = (
        lax.all_to_all(normed_one, "fsdp", split_axis=1, concat_axis=0, tiled=True),
        lax.all_to_all(attended_low, "fsdp", split_axis=1, concat_axis=0, tiled=True),
        lax.all_to_all(normed_two, "fsdp", split_axis=1, concat_axis=0, tiled=True),
        lax.all_to_all(activated, "fsdp", split_axis=1, concat_axis=0, tiled=True),
    )
    gain_shares = (
        lax.psum_scatter(grad_gain_one, "fsdp", scatter_dimension=0, tiled=True),
        lax.psum_scatter(grad_gain_two, "fsdp", scatter_dimension=0, tiled=True),
    )
    local_grads = (
        gain_shares[0],
        left_transposed(left_all[0], right_all[0]),
        left_transposed(left_all[0], right_all[1]),
        left_transposed(left_all[0], right_all[2]),
        left_transposed(left_all[1], right_all[3]),
        gain_shares[1],
        left_transposed(left_all[2], right_all[4]),
        left_transposed(left_all[2], right_all[5]),
        left_transposed(left_all[3], right_all[6]),
    )
    summed = (
        lax.psum(local_grads[0].astype(jnp.bfloat16), "ctx").astype(jnp.float32),
        lax.psum(local_grads[1].astype(jnp.bfloat16), "ctx").astype(jnp.float32),
        lax.psum(local_grads[2].astype(jnp.bfloat16), "ctx").astype(jnp.float32),
        lax.psum(local_grads[3].astype(jnp.bfloat16), "ctx").astype(jnp.float32),
        lax.psum(local_grads[4].astype(jnp.bfloat16), "ctx").astype(jnp.float32),
        lax.psum(local_grads[5].astype(jnp.bfloat16), "ctx").astype(jnp.float32),
        lax.psum(local_grads[6].astype(jnp.bfloat16), "ctx").astype(jnp.float32),
        lax.psum(local_grads[7].astype(jnp.bfloat16), "ctx").astype(jnp.float32),
        lax.psum(local_grads[8].astype(jnp.bfloat16), "ctx").astype(jnp.float32),
    )
    return (
        result_out,
        result_grad,
        summed[0],
        summed[1],
        summed[2],
        summed[3],
        summed[4],
        summed[5],
        summed[6],
        summed[7],
        summed[8],
    )


def solution(mesh):
    in_specs = (
        P("fsdp", "ctx", None),
        P("fsdp", None),
        P("fsdp"),
        P("fsdp", None),
        P("fsdp", None),
        P("fsdp", None),
        P("fsdp", None),
        P("fsdp"),
        P("fsdp", None),
        P("fsdp", None),
        P("fsdp", None),
        P("fsdp", "ctx", None),
    )
    out_specs = (
        P("fsdp", "ctx", None),
        P("fsdp", "ctx", None),
        P("fsdp"),
        P("fsdp", None),
        P("fsdp", None),
        P("fsdp", None),
        P("fsdp", None),
        P("fsdp"),
        P("fsdp", None),
        P("fsdp", None),
        P("fsdp", None),
    )
    return jax.shard_map(
        on_device, mesh=mesh, in_specs=in_specs, out_specs=out_specs, check_vma=False
    )
```

profile of v0, /device:TPU:0, one launch (start us, length us, event | category | flops | bytes accessed | tf_op | source)
XLA Modules:
  0.0 1249.6 jit_solution(6361171639691328096)
XLA Ops:
  11.6 11.3 all-reduce.7
  27.7 13.8 %all-gather.1 = bf16[4,240,320]{1,2,0:T(8,128)(2,1)S(1)} all-gather(bf16[1,240,320]{1,2,0:T(8,128)(2,1)S(1)} %bitcast.357), channel_id=1, replica_groups=mesh['fsdp'=4,'ctx'=8] {'fsdp'}, dimensions={0}, use_global_device_ids=true | all-gather | bytes 768000 | tf_op jit(solution)/shard_map/all_gather | solution.py:189
  46.2 10.5 all-gather
  77.1 10.5 all-gather.19.cloned.1.call-done
  87.6 5.5 reshape_reshape.9
  96.9 72.7 %while.39 = (s32[]{:T(128)}, f32[2,5,3,256]{3,2,1,0:T(4,128)S(1)}, f32[2,5,3,256]{3,2,1,0:T(4,128)S(1)}, s32[4,2,512]{2,1,0:T(2,128)S(1)}, s32[2,256]{1,0:T(2,12...) while((s32[]{:T(128)}, f32[2,5,3,256]{3,2,1,0:T(4,128)S(1)}, ...), condition=%wide.region_4.5_spmd.clone, body=%wide.region_1.4_spmd.clone.sunk | while | flops 531142144 | bytes 34296424 | solution.py:109
  97.2 8.9 fusion.142
  106.1 9.0 fusion.143
  115.3 8.9 fusion.142
  124.2 8.8 fusion.143
  133.4 8.9 fusion.142
  142.3 9.2 fusion.143
  151.8 8.9 fusion.142
  160.6 9.0 fusion.143
  169.7 5.5 reshape_reshape.8
  179.0 34.3 %while.40 = (s32[]{:T(128)}, f32[2,256,5,3,64]{1,4,3,2,0:T(8,128)}, bf16[4,2,512,5,64]{2,4,3,1,0:T(8,128)(2,1)}, s32[4,2,512]{2,1,0:T(2,128)S(1)}, s32[2,256]{1,...) while((s32[]{:T(128)}, f32[2,256,5,3,64]{1,4,3,2,0:T(8,128)}, ...), condition=%wide.region_6.7_spmd.clone, body=%wide.region_5.6_spmd.clone.sunk | while | flops 1023606784 | bytes 6796403 | solution.py:126
  179.7 7.7 bitcast_add_fusion.4
  187.7 8.4 bitcast_add_fusion.4
  196.3 8.4 bitcast_add_fusion.4
  204.9 8.4 bitcast_add_fusion.4
  224.3 8.3 fusion.65
  232.6 45.9 %all-gather.27.cloned.1.call-done = bf16[960,2560]{1,0:T(8,128)(2,1)} async-done(((bf16[240,2560]{1,0:T(8,128)(2,1)}), bf16[960,2560]{1,0:T(8,128)(2,1)}) %all-gather.27.cloned.1.call-update) | async-done | bytes 4915216 | tf_op jit(solution)/shard_map/all_gather | solution.py:196
  278.6 7.9 fusion.66
  286.4 52.7 %all-gather.29.cloned.1.call-done = bf16[2560,960]{0,1:T(8,128)(2,1)} async-done(((bf16[640,960]{0,1:T(8,128)(2,1)}), bf16[2560,960]{0,1:T(8,128)(2,1)}) %all-gather.29.cloned.1.call-update) | async-done | bytes 4915216 | tf_op jit(solution)/shard_map/all_gather | solution.py:197
  339.2 11.5 multiply_convert_fusion
  350.6 7.2 fusion.67
  357.8 8.1 multiply_reduce_fusion.1
  379.6 158.0 %while.41 = (s32[]{:T(128)}, f32[2,256,5,3,64]{1,4,3,2,0:T(8,128)S(1)}, bf16[4,2,512,5,64]{2,4,3,1,0:T(8,128)(2,1)}, bf16[4,2,512,5,64]{2,4,3,1,0:T(8,128)(2,1)}...) while((s32[]{:T(128)}, ...), condition=%wide.region_10.11_spmd.clone, body=%wide.region_9.10_spmd.clone.sunk | while | flops 2557968384 | bytes 119515848 | solution.py:162
  379.8 9.0 fusion.159
  389.0 8.4 fusion.160
  408.9 10.3 fusion.162
  419.1 9.0 fusion.159
  428.3 8.4 fusion.160
  448.1 10.3 fusion.162
  458.4 9.0 fusion.159
  467.6 8.4 fusion.160
  487.5 10.3 fusion.162
  497.8 9.0 fusion.159
  507.0 8.4 fusion.160
  521.9 5.0 bitcast_add_fusion.5
  526.9 10.3 fusion.162
  537.6 5.2 copy.126
  542.8 5.5 convert_element_type.207
  548.4 5.3 copy.128
  553.7 5.5 convert_element_type.211
  567.8 18.3 %reduce-scatter.3.cloned.1.call-done = bf16[2,256,320]{1,2,0:T(8,128)(2,1)} async-done(((bf16[2,2048,320]{1,2,0:T(8,128)(2,1)}), bf16[2,256,320]{1,2,0:T(8,128)(2,1)}) %reduce-scatter.3.cloned.1.call-update) | async-done | bytes 327696 | tf_op jit(solution)/shard_map/reduce_scatter | solution.py:246
  588.8 36.0 %reduce-scatter.5.cloned.1.call-done = bf16[2,256,320]{1,2,0:T(8,128)(2,1)} async-done(((bf16[2,2048,320]{1,2,0:T(8,128)(2,1)}), bf16[2,256,320]{1,2,0:T(8,128)(2,1)}) %reduce-scatter.5.cloned.1.call-update) | async-done | bytes 327696 | tf_op jit(solution)/shard_map/reduce_scatter | solution.py:252
  639.4 18.2 %all-to-all-done = bf16[512,4,240]{0,2,1:T(8,128)(2,1)S(1)} async-done(((bf16[512,4,240]{0,2,1:T(8,128)(2,1)}), bf16[512,4,240]{0,2,1:T(8,128)(2,1)S(1)}, u32[]{:S(2)}, u32[]{:S(2)}) %all-to-all-start) | async-done | bytes 983072 | tf_op jit(solution)/shard_map/all_to_all | solution.py:283
  657.6 25.9 %all_to_all.73 = bf16[512,4,240]{0,2,1:T(8,128)(2,1)S(1)} all-to-all(bf16[512,4,240]{0,2,1:T(8,128)(2,1)} %all_to_all.57), channel_id=1, replica_groups=mesh['fsdp'=4,'ctx'=8] {'fsdp'}, dimensions={1} | all-to-all | bytes 1966080 | tf_op jit(solution)/shard_map/all_to_all | solution.py:284
  690.5 14.5 %all-to-all-done.2 = bf16[512,4,240]{0,2,1:T(8,128)(2,1)S(1)} async-done(((bf16[512,4,240]{0,2,1:T(8,128)(2,1)}), bf16[512,4,240]{0,2,1:T(8,128)(2,1)S(1)}, u32[]{:S(2)}, u32[]{:S(2)}) %all-to-all-start.2) | async-done | bytes 983072 | tf_op jit(solution)/shard_map/all_to_all | solution.py:285
  717.2 32.3 %all-to-all-done.3 = bf16[512,4,640]{2,0,1:T(8,128)(2,1)} async-done(((bf16[512,4,640]{2,0,1:T(8,128)(2,1)}), bf16[512,4,640]{2,0,1:T(8,128)(2,1)}, u32[]{:S(2)}, u32[]{:S(2)}) %all-to-all-start.3) | async-done | bytes 2621472 | tf_op jit(solution)/shard_map/all_to_all | solution.py:286
  749.5 7.4 convolution_convert_fusion.2
  756.9 24.9 %all-gather.37.cloned.1.call-done = bf16[2048,960]{0,1:T(8,128)(2,1)} async-done(((bf16[512,960]{0,1:T(8,128)(2,1)}), bf16[2048,960]{0,1:T(8,128)(2,1)}) %all-gather.37.cloned.1.call-update) | async-done | bytes 3932176 | tf_op jit(solution)/shard_map/all_gather | solution.py:277
  786.1 48.4 %all-gather.31.cloned.1.call-done = bf16[2048,960]{0,1:T(8,128)(2,1)} async-done(((bf16[512,960]{0,1:T(8,128)(2,1)}), bf16[2048,960]{0,1:T(8,128)(2,1)}) %all-gather.31.cloned.1.call-update) | async-done | bytes 3932176 | tf_op jit(solution)/shard_map/all_gather | solution.py:274
  838.6 26.9 %all-gather.33.cloned.1.call-done = bf16[2048,320]{0,1:T(8,128)(2,1)} async-done(((bf16[512,320]{0,1:T(8,128)(2,1)}), bf16[2048,320]{0,1:T(8,128)(2,1)}) %all-gather.33.cloned.1.call-update) | async-done | bytes 1310736 | tf_op jit(solution)/shard_map/all_gather | solution.py:275
  868.0 28.4 %all-gather.35.cloned.1.call-done = bf16[2048,320]{0,1:T(8,128)(2,1)} async-done(((bf16[512,320]{0,1:T(8,128)(2,1)}), bf16[2048,320]{0,1:T(8,128)(2,1)}) %all-gather.35.cloned.1.call-update) | async-done | bytes 1310736 | tf_op jit(solution)/shard_map/all_gather | solution.py:276
  899.0 104.3 %all-gather.41.cloned.1.call-done = bf16[2048,2560]{1,0:T(8,128)(2,1)} async-done(((bf16[512,2560]{1,0:T(8,128)(2,1)}), bf16[2048,2560]{1,0:T(8,128)(2,1)}) %all-gather.41.cloned.1.call-update) | async-done | bytes 10485776 | tf_op jit(solution)/shard_map/all_gather | solution.py:279
  1003.3 7.7 convolution_convert_fusion
  1011.0 99.1 %all-gather.39.cloned.1.call-done = bf16[2048,2560]{1,0:T(8,128)(2,1)} async-done(((bf16[512,2560]{1,0:T(8,128)(2,1)}), bf16[2048,2560]{1,0:T(8,128)(2,1)}) %all-gather.39.cloned.1.call-update) | async-done | bytes 10485776 | tf_op jit(solution)/shard_map/all_gather | solution.py:278
  1110.1 7.7 convolution_convert_fusion.1
  1119.3 7.0 add_convert_fusion.1
  1130.8 9.1 all-reduce.4
  1140.0 15.6 %all-reduce.5 = (bf16[240]{0:T(256)(128)(2,1)S(1)}, bf16[240]{0:T(256)(128)(2,1)S(1)}) all-reduce(bf16[240]{0:T(256)(128)(2,1)S(1)} %dynamic-slice.9, bf16[240]{0:T(256)(128)(2,1)S(1)} %dynamic-slice.8), channel_id=1, replica_groups=mesh['fsdp'=4,'ctx'=8] {'ctx'}, use_global_device_ids=true, to_apply=%region_16.17 | all-reduce | flops 480 | bytes 1920 | tf_op jit(solution)/shard_map/psum | solution.py:304
  1162.0 70.8 %all-reduce.10.cloned.1.call-done = (bf16[240,960]{1,0:T(8,128)(2,1)}, bf16[240,320]{0,1:T(8,128)(2,1)}, bf16[240,320]{0,1:T(8,128)(2,1)}, bf16[240,960]{1,0:T(8...) async-done(((bf16[240,960]{1,0:T(8,128)(2,1)}, bf16[240,320]{0,1:T(8,128)(2,1)}, bf16[240,320]{0,1:T(8,128)(2,1)}, ...) | async-done | bytes 4915216 | tf_op jit(solution)/shard_map/psum | solution.py:305
  (317 shorter events, 188.7 us)
Async XLA Ops:
  7.2 57.0 %all-gather.21.cloned.1.call-start = ((), (), s32[]{:S(2)}) async-start(), calls=%async_computation.8 | async-start | bytes 2457600 | tf_op jit(solution)/shard_map/all_gather | solution.py:188
  7.9 79.7 %all-gather.19.cloned.1.call-start = ((), (), s32[]{:S(2)}) async-start(), calls=%async_computation.7 | async-start | bytes 2949120 | tf_op jit(solution)/shard_map/all_gather | solution.py:212
  23.0 34.8 %copy-start.45 = (f32[960]{0:T(1024)}, f32[960]{0:T(1024)S(1)}, u32[]{:S(2)}) copy-start(f32[960]{0:T(1024)S(1)} %convert_element_type.186) | copy-start | bytes 11524
  27.6 16.3 %copy-start.32 = (bf16[512,960,1]{0,1,2:T(8,128)(2,1)}, bf16[512,960,1]{0,1,2:T(8,128)(2,1)S(1)}, u32[]{:S(2)}) copy-start(bf16[512,960,1]{0,1,2:T(8,128)(2,1)S(1)} %reshape.311) | copy-start | bytes 2949124
  42.8 28.0 %copy-start.26 = (f32[512,32]{0,1:T(8,128)}, f32[512,32]{0,1:T(8,128)S(1)}, u32[]{:S(2)}) copy-start(f32[512,32]{0,1:T(8,128)S(1)} %get-tuple-element.482) | copy-start | bytes 196612
  42.8 28.0 %copy-start.28 = (f32[512,32]{0,1:T(8,128)}, f32[512,32]{0,1:T(8,128)S(1)}, u32[]{:S(2)}) copy-start(f32[512,32]{0,1:T(8,128)S(1)} %get-tuple-element.483) | copy-start | bytes 196612
  44.9 124.8 %all-gather.17.cloned.1.call-start = ((), (), s32[]{:S(2)}) async-start(), calls=%async_computation.6 | async-start | bytes 2949120 | tf_op jit(solution)/shard_map/all_gather | solution.py:213
  45.1 12.7 %copy-start.47 = (f32[1,2,2,128]{3,1,2,0:T(2,128)}, f32[1,2,2,128]{3,1,2,0:T(2,128)S(1)}, u32[]{:S(2)}) copy-start(f32[1,2,2,128]{3,1,2,0:T(2,128)S(1)} %copy.165) | copy-start | bytes 6148
  45.5 12.9 %copy-start.1 = (f32[2,120,8,256]{3,2,0,1:T(8,128)}, f32[2,120,8,256]{3,2,0,1:T(8,128)S(1)}, u32[]{:S(2)}) copy-start(f32[2,120,8,256]{3,2,0,1:T(8,128)S(1)} %copy.159) | copy-start | bytes 5898244
  57.7 2.6 copy-start.15
  59.1 159.0 %all-gather.23.cloned.1.call-start = ((), (), s32[]{:S(2)}) async-start(), calls=%async_computation.9 | async-start | bytes 2457600 | tf_op jit(solution)/shard_map/all_gather | solution.py:191
  59.7 164.6 %all-gather.25.cloned.1.call-start = ((), (), s32[]{:S(2)}) async-start(), calls=%async_computation.10 | async-start | bytes 6144000 | tf_op jit(solution)/shard_map/all_gather | solution.py:195
  60.3 218.3 %all-gather.27.cloned.1.call-start = ((), (), s32[]{:S(2)}) async-start(), calls=%async_computation.11 | async-start | bytes 6144000 | tf_op jit(solution)/shard_map/all_gather | solution.py:196
  60.9 278.3 %all-gather.29.cloned.1.call-start = ((), (), s32[]{:S(2)}) async-start(), calls=%async_computation.12 | async-start | bytes 6144000 | tf_op jit(solution)/shard_map/all_gather | solution.py:197
  61.6 524.4 %reduce-scatter.3.cloned.1.call-start = ((), (), s32[]{:S(2)}) async-start(), calls=%async_computation.13 | async-start | bytes 2949120 | tf_op jit(solution)/shard_map/reduce_scatter | solution.py:246
  62.0 304.0 %copy-start.49 = (f32[960]{0:T(1024)}, f32[960]{0:T(1024)S(1)}, u32[]{:S(2)}) copy-start(f32[960]{0:T(1024)S(1)} %convert_element_type.195) | copy-start | bytes 11524
  64.2 3.9 copy-start.33
  221.9 144.1 %copy-start.51 = (f32[512]{0:T(512)}, f32[512]{0:T(512)S(1)}, u32[]{:S(2)}) copy-start(f32[512]{0:T(512)S(1)} %get-tuple-element.485) | copy-start | bytes 6148
  221.9 144.1 %copy-start.53 = (f32[512]{0:T(512)}, f32[512]{0:T(512)S(1)}, u32[]{:S(2)}) copy-start(f32[512]{0:T(512)S(1)} %get-tuple-element.484) | copy-start | bytes 6148
  357.8 9.4 copy-start.4
  357.8 9.4 copy-start.8
  366.0 2.8 copy-start.55
  375.9 3.3 copy-start.13
  379.8 9.2 copy-start.34
  397.4 3.1 copy-start
  419.1 9.2 copy-start.34
  436.8 3.1 copy-start
  458.4 9.2 copy-start.34
  476.1 3.1 copy-start
  497.8 9.2 copy-start.34
  515.4 3.1 copy-start
  548.4 76.5 %reduce-scatter.5.cloned.1.call-start = ((), (), s32[]{:S(2)}) async-start(), calls=%async_computation.14 | async-start | bytes 2949120 | tf_op jit(solution)/shard_map/reduce_scatter | solution.py:252
  559.3 157.9 %all-gather.43.cloned.1.call-start = ((), (), s32[]{:S(2)}) async-start(), calls=%async_computation.21 | async-start | bytes 4915200 | tf_op jit(solution)/shard_map/all_gather | solution.py:280
  559.9 221.9 %all-gather.37.cloned.1.call-start = ((), (), s32[]{:S(2)}) async-start(), calls=%async_computation.18 | async-start | bytes 4915200 | tf_op jit(solution)/shard_map/all_gather | solution.py:277
  560.6 273.8 %all-gather.31.cloned.1.call-start = ((), (), s32[]{:S(2)}) async-start(), calls=%async_computation.15 | async-start | bytes 4915200 | tf_op jit(solution)/shard_map/all_gather | solution.py:274
  563.4 2.9 copy-start.27
  563.4 2.9 copy-start.29
  567.7 297.8 %all-gather.33.cloned.1.call-start = ((), (), s32[]{:S(2)}) async-start(), calls=%async_computation.16 | async-start | bytes 1638400 | tf_op jit(solution)/shard_map/all_gather | solution.py:275
  588.8 307.7 %all-gather.35.cloned.1.call-start = ((), (), s32[]{:S(2)}) async-start(), calls=%async_computation.17 | async-start | bytes 1638400 | tf_op jit(solution)/shard_map/all_gather | solution.py:276
  626.6 376.7 %all-gather.41.cloned.1.call-start = ((), (), s32[]{:S(2)}) async-start(), calls=%async_computation.20 | async-start | bytes 13107200 | tf_op jit(solution)/shard_map/all_gather | solution.py:279
  627.2 482.9 %all-gather.39.cloned.1.call-start = ((), (), s32[]{:S(2)}) async-start(), calls=%async_computation.19 | async-start | bytes 13107200 | tf_op jit(solution)/shard_map/all_gather | solution.py:278
  630.2 2.9 copy-start.48
  633.0 4.8 copy-start.11
  634.2 23.4 %all-to-all-start = ((bf16[512,4,240]{0,2,1:T(8,128)(2,1)}), bf16[512,4,240]{0,2,1:T(8,128)(2,1)S(1)}, u32[]{:S(2)}, u32[]{:S(2)}) async-start(bf16[512,4,240]{0,2,1:T(8,128)(2,1)} %multiply_convert_fusion.3), calls=%async_computation.2 | async-start | bytes 1966080 | tf_op jit(solution)/shard_map/all_to_all | solution.py:283
  683.5 21.5 %all-to-all-start.2 = ((bf16[512,4,240]{0,2,1:T(8,128)(2,1)}), bf16[512,4,240]{0,2,1:T(8,128)(2,1)S(1)}, u32[]{:S(2)}, u32[]{:S(2)}) async-start(bf16[512,4,240]{0,2,1:T(8,128)(2,1)} %bitcast.20), calls=%async_computation.4 | async-start | bytes 1966080 | tf_op jit(solution)/shard_map/all_to_all | solution.py:285
  706.0 43.5 %all-to-all-start.3 = ((bf16[512,4,640]{2,0,1:T(8,128)(2,1)}), bf16[512,4,640]{2,0,1:T(8,128)(2,1)}, u32[]{:S(2)}, u32[]{:S(2)}) async-start(bf16[512,4,640]{2,0,1:T(8,128)(2,1)} %bitcast.260), calls=%async_computation.5 | async-start | bytes 5242880 | tf_op jit(solution)/shard_map/all_to_all | solution.py:286
  710.5 522.2 %all-reduce.10.cloned.1.call-start = ((), (), s32[]{:S(2)}) async-start(), calls=%async_computation.22 | async-start | bytes 9994240 | tf_op jit(solution)/shard_map/psum | solution.py:305
  749.5 32.2 %copy-start.36 = (bf16[4,30,8,512]{3,2,0,1:T(8,128)(2,1)S(1)}, bf16[4,30,8,512]{3,2,0,1:T(8,128)(2,1)}, u32[]{:S(2)}) copy-start(bf16[4,30,8,512]{3,2,0,1:T(8,128)(2,1)} %copy.163) | copy-start | bytes 2949124
  781.8 52.7 %copy-start.35 = (bf16[4,30,8,512]{3,2,0,1:T(8,128)(2,1)S(1)}, bf16[4,30,8,512]{3,2,0,1:T(8,128)(2,1)}, u32[]{:S(2)}) copy-start(bf16[4,30,8,512]{3,2,0,1:T(8,128)(2,1)} %copy.162) | copy-start | bytes 2949124
  1119.3 7.0 copy-start.21
  1119.3 7.0 copy-start.23
  1119.3 7.8 copy-start.25
  1119.3 7.8 copy-start.46
  1128.1 2.6 copy-start.59
  1128.1 28.6 %copy-start.9 = (bf16[2,120,8,256]{3,2,0,1:T(8,128)(2,1)S(1)}, bf16[2,120,8,256]{3,2,0,1:T(8,128)(2,1)}, u32[]{:S(2)}) copy-start(bf16[2,120,8,256]{3,2,0,1:T(8,128)(2,1)} %copy.160) | copy-start | bytes 2949124
  1128.3 28.4 %copy-start.50 = (f32[960]{0:T(1024)S(1)}, f32[960]{0:T(1024)}, u32[]{:S(2)}) copy-start(f32[960]{0:T(1024)} %copy-done.49) | copy-start | bytes 11524
  1128.3 28.4 %copy-start.52 = (f32[512]{0:T(512)S(1)}, f32[512]{0:T(512)}, u32[]{:S(2)}) copy-start(f32[512]{0:T(512)} %copy-done.51) | copy-start | bytes 6148
  1128.3 28.4 %copy-start.54 = (f32[512]{0:T(512)S(1)}, f32[512]{0:T(512)}, u32[]{:S(2)}) copy-start(f32[512]{0:T(512)} %copy-done.53) | copy-start | bytes 6148
  1128.3 28.4 %copy-start.56 = (f32[512]{0:T(512)S(1)}, f32[512]{0:T(512)}, u32[]{:S(2)}) copy-start(f32[512]{0:T(512)} %copy-done.55) | copy-start | bytes 6148
  1156.7 3.8 copy-start.37
  1232.8 3.1 copy-start.31
  1237.6 2.7 copy-start.38
  1237.6 3.7 copy-start.44
  1239.2 2.9 copy-start.43
  (22 other events, 32.9 us)
Sparse Core Ops, SparseCore 0:
  9.9 40.3 all-gather.20
  52.4 35.1 all-gather.18
  89.8 33.3 all-gather.16
  124.9 32.7 all-gather.22
  159.4 58.6 all-gather.24
  219.8 58.6 all-gather.26
  280.4 58.6 all-gather.28
  548.5 37.5 reduce-scatter.2
  588.4 36.4 reduce-scatter.4
  627.1 78.1 all-gather.42
  707.7 74.0 all-gather.36
  784.0 50.3 all-gather.30
  836.8 28.6 all-gather.32
  867.8 28.6 all-gather.34
  898.2 105.0 all-gather.40
  1005.0 105.0 all-gather.38
  1117.9 114.7 all-reduce.9
where the time goes:
time: 1260 us; the launch traced here: 1250 us
  waiting for transfers between devices  637 us (51%)
  matrix products  316 us (25%)
  local copies, waits for them, and re-layouts  112 us (9%)
  blocking collectives  86.2 us (7%)
  other arithmetic  68.6 us (5%)
  between operations  16.6 us (1%)
  starting transfers between devices  12.7 us (1%)
    all_gather x1, waiting for transfers between devices, on_device(): lax.all_gather(grad_upper, 'fsdp', axis=0, tiled=True)  104 us
    all_gather x1, waiting for transfers between devices, on_device(): lax.all_gather(grad_gate, 'fsdp', axis=0, tiled=True)  99.1 us
    dot_general x8, matrix products, block_scores(): jnp.einsum('rgah,kgh->gark', query, key_block, preferred_element_type=jnp...  71.3 us
    psum x1, waiting for transfers between devices, on_device(): lax.psum(local_grads[1].astype(jnp.bfloat16), 'ctx').astype(jnp.float32)  70.8 us
    all_gather x1, waiting for transfers between devices, on_device(): lax.all_gather(w_down, 'fsdp', axis=0, tiled=True)  52.7 us
    all_gather x1, waiting for transfers between devices, on_device(): lax.all_gather(grad_query_low, 'fsdp', axis=0, tiled=True)  48.4 us
    all_gather x1, waiting for transfers between devices, on_device(): lax.all_gather(w_up, 'fsdp', axis=0, tiled=True)  45.9 us
    dot_general x4, matrix products, accumulate(): jnp.einsum('gark,rgah->kgh', rounded, upstream, preferred_element_type=jn...  41.1 us
  transfers between devices with their start and end apart: 20, of which 15 were waited for; matrix products, arithmetic and copies ran while one was open for 21% of the time, Pallas kernels for 0%

commit v1 on v0

v1 whole, which is shorter than its diff:
```python
import math

import jax
import jax.numpy as jnp
from jax import lax
from jax.experimental import pallas as pl
from jax.experimental.pallas import tpu as pltpu
from jax.sharding import PartitionSpec as P

HEADS = 15
KV_HEADS = 5
HEAD = 64


epsilon = 1e-05
rope_log_base = math.log(100000.0)
masked_value = -1e30


def matmul(left, right):
    return jnp.dot(left, right, preferred_element_type=jnp.float32)


def left_transposed(left, right):
    return lax.dot_general(
        left, right, (((0,), (0,)), ((), ())), preferred_element_type=jnp.float32
    )


def right_transposed(left, right):
    return lax.dot_general(
        left, right, (((1,), (1,)), ((), ())), preferred_element_type=jnp.float32
    )


def angle_tables(places):
    half = HEAD // 2
    freqs = jnp.exp(-rope_log_base * (2.0 * jnp.arange(half, dtype=jnp.float32) / HEAD))
    angles = places.astype(jnp.float32)[..., None] * freqs
    cosine, sine = jnp.cos(angles), jnp.sin(angles)
    return (
        jnp.concatenate([cosine, cosine], axis=-1),
        jnp.concatenate([-sine, sine], axis=-1),
    )


def swap_halves(values):
    half = HEAD // 2
    return jnp.concatenate([values[:, half:], values[:, :half]], axis=1)


def turn(values, cosine, sine):
    half = HEAD // 2
    heads = values.shape[1] // HEAD
    lane = lax.broadcasted_iota(jnp.int32, values.shape, 1)
    swapped = jnp.where(
        lax.rem(lane, HEAD) < half, jnp.roll(values, -half, axis=1), jnp.roll(values, half, axis=1)
    )
    return values * jnp.tile(cosine, (1, heads)) + swapped * jnp.tile(sine, (1, heads))


def norm_forward(values, gain):
    inverse_scale = lax.rsqrt(jnp.mean(values * values, axis=1, keepdims=True) + epsilon)
    return (values * inverse_scale * gain, inverse_scale)


def norm_backward(values, inverse_scale, gain, upstream):
    scaled = gain * upstream
    inner = jnp.mean(scaled * values, axis=1, keepdims=True)
    grad_values = (
        inverse_scale * scaled - values * (inverse_scale * inverse_scale * inverse_scale) * inner
    )
    grad_gain = jnp.sum(upstream * values * inverse_scale, axis=0)
    return (grad_values, grad_gain)


def contract_last(left, right):
    return lax.dot_general(
        left, right, (((1,), (1,)), ((), ())), preferred_element_type=jnp.float32
    )


def forward_kernel(
    raw_ref, key_ref, value_ref, own_ref, place_ref, cos_ref, sin_ref, query_ref, out_ref, lse_ref, bias_ref
):
    groups = HEADS // KV_HEADS
    bias_ref[...] = jnp.where(place_ref[0] <= own_ref[0], 0.0, masked_value)
    cosine, sine = cos_ref[0], sin_ref[0]
    length = key_ref.shape[1]
    for kv in range(KV_HEADS):
        kv_lanes = slice(kv * HEAD, (kv + 1) * HEAD)
        keys = key_ref[0, :, kv_lanes]
        values = value_ref[0, :, kv_lanes].astype(jnp.float32).T.astype(jnp.bfloat16)
        values = jnp.concatenate([values, jnp.ones((16, length), jnp.bfloat16)], axis=0)
        for head in range(kv * groups, (kv + 1) * groups):
            lanes = slice(head * HEAD, (head + 1) * HEAD)
            raw = raw_ref[0, :, lanes]
            query = (raw * cosine + swap_halves(raw) * sine).astype(jnp.bfloat16)
            query_ref[0, :, lanes] = query
            logits = contract_last(keys, query * 0.125) + bias_ref[...]
            peak = jnp.max(logits, axis=0, keepdims=True)
            terms = jnp.exp(logits - peak).astype(jnp.bfloat16)
            summed = matmul(values, terms)
            total = summed[HEAD : HEAD + 1]
            lse_ref[0, head : head + 1, :] = peak + jnp.log(total)
            out_ref[0, :, lanes] = (summed[:HEAD] / total).T.astype(jnp.bfloat16)


def backward_kernel(
    query_ref, up_ref, out_ref, key_ref, value_ref, own_ref, place_ref, cos_ref, sin_ref, lse_ref,
    grad_query_ref, grad_key_ref, grad_value_ref, bias_ref,
):
    groups = HEADS // KV_HEADS
    rows = query_ref.shape[1]
    length = key_ref.shape[1]
    block = min(512, length)
    one = jnp.where(place_ref[0] <= own_ref[0], 0.0, masked_value)
    bias_ref[...] = jnp.concatenate([one] * groups, axis=1)
    cosine, sine = cos_ref[0], sin_ref[0]
    for kv in range(KV_HEADS):
        kv_lanes = slice(kv * HEAD, (kv + 1) * HEAD)
        heads = range(kv * groups, (kv + 1) * groups)
        queries, ups, shifts, deltas = [], [], [], []
        for head in heads:
            lanes = slice(head * HEAD, (head + 1) * HEAD)
            up = up_ref[0, :, lanes]
            product = up.astype(jnp.float32) * out_ref[0, :, lanes].astype(jnp.float32)
            queries.append(query_ref[0, :, lanes] * 0.125)
            ups.append(up)
            shifts.append(lse_ref[0, head : head + 1, :])
            deltas.append(jnp.sum(product.T, axis=0, keepdims=True))
        query = jnp.concatenate(queries, axis=0)
        upstream = jnp.concatenate(ups, axis=0)
        shift = jnp.concatenate(shifts, axis=1)
        delta = jnp.concatenate(deltas, axis=1)
        total = jnp.zeros((HEAD, groups * rows), jnp.float32)
        for start in range(0, length, block):
            span = slice(start, start + block)
            keys = key_ref[0, span, kv_lanes]
            values = value_ref[0, span, kv_lanes]
            logits = contract_last(keys, query) + bias_ref[span, :]
            weights = jnp.exp(logits - shift)
            grad_weights = contract_last(values, upstream)
            grad_logits = (weights * (grad_weights - delta)).astype(jnp.bfloat16)
            grad_value = matmul(weights.astype(jnp.bfloat16), upstream)
            grad_key = matmul(grad_logits, query)
            grad_value_ref[0, span, kv_lanes] = grad_value.astype(jnp.bfloat16)
            grad_key_ref[0, span, kv_lanes] = grad_key.astype(jnp.bfloat16)
            total += matmul(keys.astype(jnp.float32).T.astype(jnp.bfloat16), grad_logits)
        total = total * 0.125
        for at, head in enumerate(heads):
            grad = total[:, at * rows : (at + 1) * rows].T
            grad = grad * cosine - swap_halves(grad) * sine
            grad_query_ref[0, :, head * HEAD : (head + 1) * HEAD] = grad.astype(jnp.bfloat16)


def whole_block(array):
    return pl.BlockSpec((1,) + array.shape[1:], lambda at: (at, 0, 0))


def attend_forward(raw, keys, values, own_places, places, cosine, sine):
    seqs, rows, width = raw.shape
    length = keys.shape[1]
    operands = (raw, keys, values, own_places[:, None, :], places[:, :, None], cosine, sine)
    outs = (
        jax.ShapeDtypeStruct(raw.shape, jnp.bfloat16),
        jax.ShapeDtypeStruct(raw.shape, jnp.bfloat16),
        jax.ShapeDtypeStruct((seqs, HEADS, rows), jnp.float32),
    )
    pairs = seqs * rows * length * HEADS
    return pl.pallas_call(
        forward_kernel,
        grid=(seqs,),
        in_specs=[whole_block(array) for array in operands],
        out_specs=[whole_block(array) for array in outs],
        out_shape=outs,
        scratch_shapes=[pltpu.VMEM((length, rows), jnp.float32)],
        compiler_params=pltpu.CompilerParams(vmem_limit_bytes=48 * 1024 * 1024),
        cost_estimate=pl.CostEstimate(
            flops=8 * pairs * HEAD, bytes_accessed=4 * raw.size * 3, transcendentals=pairs
        ),
    )(*operands)


def attend_backward(query, upstream, output, keys, values, own_places, places, cosine, sine, lse):
    seqs, rows, width = query.shape
    length = keys.shape[1]
    operands = (
        query, upstream, output, keys, values,
        own_places[:, None, :], places[:, :, None], cosine, sine, lse,
    )
    outs = (
        jax.ShapeDtypeStruct(query.shape, jnp.bfloat16),
        jax.ShapeDtypeStruct(keys.shape, jnp.bfloat16),
        jax.ShapeDtypeStruct(values.shape, jnp.bfloat16),
    )
    pairs = seqs * rows * length * HEADS
    return pl.pallas_call(
        backward_kernel,
        grid=(seqs,),
        in_specs=[whole_block(array) for array in operands],
        out_specs=[whole_block(array) for array in outs],
        out_shape=outs,
        scratch_shapes=[pltpu.VMEM((length, rows * (HEADS // KV_HEADS)), jnp.float32)],
        compiler_params=pltpu.CompilerParams(vmem_limit_bytes=56 * 1024 * 1024),
        cost_estimate=pl.CostEstimate(
            flops=20 * pairs * HEAD, bytes_accessed=4 * query.size * 3, transcendentals=pairs
        ),
    )(*operands)


def half_of(array, which):
    size = array.shape[1] // 2
    return lax.dynamic_slice_in_dim(array, which * size, size, 1)


def core_swap(array):
    count = lax.axis_size("ctx")
    return lax.ppermute(array, "ctx", [(at, at ^ 1) for at in range(count)])


def join_halves(mine, other, which):
    first = which == 0
    return jnp.concatenate(
        [jnp.where(first, mine, other), jnp.where(first, other, mine)], axis=1
    )


def gather_weight(shard, which):
    mine = lax.all_gather(half_of(shard, which), "fsdp", axis=0, tiled=True)
    return join_halves(mine, core_swap(mine), which)


def start_share(left, right, which):
    theirs = left_transposed(left, half_of(right, 1 - which)).astype(jnp.bfloat16)
    got = core_swap(theirs).astype(jnp.float32)
    mine = left_transposed(left, half_of(right, which)) + got
    return mine.astype(jnp.bfloat16)


def scatter_share(mine):
    return lax.psum_scatter(mine, "fsdp", scatter_dimension=0, tiled=True)


def sum_share(part, which):
    count = lax.axis_size("ctx")
    groups = [list(range(0, count, 2)), list(range(1, count, 2))]
    mine = lax.psum(part, "ctx", axis_index_groups=groups)
    return join_halves(mine, core_swap(mine), which).astype(jnp.float32)


def on_device(
    x_in,
    positions,
    norm_one,
    w_query,
    w_key,
    w_value,
    w_output,
    norm_two,
    w_gate,
    w_up,
    w_down,
    cotangent,
):
    seqs, rows, width = x_in.shape
    total_rows = seqs * rows
    kv_width = KV_HEADS * HEAD
    which = lax.rem(lax.axis_index("ctx"), 2)
    at_key, at_value = width, width + kv_width
    at_gain = width + 2 * kv_width
    padded = -(-(at_gain + 2) // 256) * 256
    packed = jnp.concatenate(
        [
            w_query,
            w_key,
            w_value,
            norm_one[:, None],
            norm_two[:, None],
            jnp.zeros((w_query.shape[0], padded - at_gain - 2), jnp.bfloat16),
        ],
        axis=1,
    )
    packed = gather_weight(packed, which)
    query_w, key_w = packed[:, :at_key], packed[:, at_key:at_value]
    value_w = packed[:, at_value:at_gain]
    gain_one, gain_two = packed[:, at_gain], packed[:, at_gain + 1]
    output_w = gather_weight(w_output, which)
    gate_w = gather_weight(w_gate, which)
    up_w = gather_weight(w_up, which)
    down_w = gather_weight(w_down, which)
    own_places = lax.dynamic_slice_in_dim(positions, lax.axis_index("ctx") * rows, rows, 1)
    table_cos, table_sin = angle_tables(own_places)
    cosine, sine = table_cos.reshape(total_rows, HEAD), table_sin.reshape(total_rows, HEAD)
    inputs = x_in.reshape(total_rows, width).astype(jnp.float32)
    first_gain = gain_one.astype(jnp.float32)
    normed, first_scale = norm_forward(inputs, first_gain)
    normed_one = normed.astype(jnp.bfloat16)
    raw_query = matmul(normed_one, query_w).reshape(seqs, rows, width)
    own_keys = turn(matmul(normed_one, key_w), cosine, sine)
    own_keys = own_keys.astype(jnp.bfloat16).reshape(seqs, rows, kv_width)
    own_values = matmul(normed_one, value_w).astype(jnp.bfloat16).reshape(seqs, rows, kv_width)
    all_keys, all_values = (
        lax.all_gather(own_keys, "ctx", axis=1, tiled=True),
        lax.all_gather(own_values, "ctx", axis=1, tiled=True),
    )
    query, attended, lse = attend_forward(
        raw_query, all_keys, all_values, own_places, positions, table_cos, table_sin
    )
    attended_low = attended.reshape(total_rows, HEADS * HEAD)
    hidden = inputs + matmul(attended_low, output_w)
    second_gain = gain_two.astype(jnp.float32)
    normed, second_scale = norm_forward(hidden, second_gain)
    normed_two = normed.astype(jnp.bfloat16)
    gate = matmul(normed_two, gate_w)
    upper = matmul(normed_two, up_w)
    sigmoid = jax.nn.sigmoid(gate)
    activated = (gate * sigmoid * upper).astype(jnp.bfloat16)
    output = hidden + matmul(activated, down_w)
    upstream = cotangent.reshape(total_rows, width)
    grad_act = right_transposed(upstream, down_w)
    grad_gate = (grad_act * upper * sigmoid * (1.0 + gate * (1.0 - sigmoid))).astype(jnp.bfloat16)
    grad_upper = (grad_act * gate * sigmoid).astype(jnp.bfloat16)
    grad_normed_two = right_transposed(grad_gate, gate_w) + right_transposed(grad_upper, up_w)
    grad_hidden, grad_gain_two = norm_backward(hidden, second_scale, second_gain, grad_normed_two)
    grad_hidden = grad_hidden + upstream.astype(jnp.float32)
    grad_branch = grad_hidden.astype(jnp.bfloat16)
    grad_attended = right_transposed(grad_branch, output_w).astype(jnp.bfloat16)
    early = tuple(
        start_share(left, right, which)
        for left, right in (
            (activated, upstream),
            (normed_two, grad_gate),
            (normed_two, grad_upper),
            (attended_low, grad_branch),
        )
    )
    grad_attended, early = lax.optimization_barrier((grad_attended, early))
    first_part = scatter_share(early[0])
    grad_query, grad_keys, grad_values = attend_backward(
        query, grad_attended.reshape(seqs, rows, width), attended, all_keys, all_values,
        own_places, positions, table_cos, table_sin, lse,
    )
    grad_keys, grad_values, first_part = lax.optimization_barrier(
        (grad_keys, grad_values, first_part)
    )
    own_grad_keys, own_grad_values = (
        lax.psum_scatter(
            grad_keys,
            "ctx",
            scatter_dimension=1,
            tiled=True,
        ).astype(jnp.float32),
        lax.psum_scatter(
            grad_values,
            "ctx",
            scatter_dimension=1,
            tiled=True,
        ).astype(jnp.float32),
    )
    grad_query_low = grad_query.reshape(total_rows, HEADS * HEAD)
    grad_key_low = turn(own_grad_keys.reshape(total_rows, kv_width), cosine, -sine)
    grad_key_low = grad_key_low.astype(jnp.bfloat16)
    grad_value_low = own_grad_values.reshape(total_rows, kv_width).astype(jnp.bfloat16)
    grad_normed_one = (
        right_transposed(grad_query_low, query_w)
        + right_transposed(grad_key_low, key_w)
        + right_transposed(grad_value_low, value_w)
    )
    grad_inputs, grad_gain_one = norm_backward(inputs, first_scale, first_gain, grad_normed_one)
    grad_inputs = grad_inputs + grad_hidden
    result_out = output.astype(jnp.bfloat16).reshape(seqs, rows, width)
    result_grad = grad_inputs.astype(jnp.bfloat16).reshape(seqs, rows, width)
    own_grad_keys, own_grad_values, rest = lax.optimization_barrier(
        (own_grad_keys, own_grad_values, early[1:])
    )
    parts = (first_part,) + tuple(scatter_share(share) for share in rest)
    rights = jnp.concatenate(
        [
            grad_query_low,
            grad_key_low,
            grad_value_low,
            jnp.zeros((total_rows, padded - at_gain), jnp.bfloat16),
        ],
        axis=1,
    )
    late = start_share(normed_one, rights, which)
    late_part = scatter_share(late)
    sums = tuple(sum_share(part, which) for part in parts)
    late_sum = sum_share(late_part, which)
    gains = lax.psum(jnp.stack([grad_gain_one, grad_gain_two]), ("fsdp", "ctx"))
    own_rows = norm_one.shape[0]
    gains = lax.dynamic_slice_in_dim(gains, lax.axis_index("fsdp") * own_rows, own_rows, 1)
    return (
        result_out,
        result_grad,
        gains[0],
        late_sum[:, :at_key],
        late_sum[:, at_key:at_value],
        late_sum[:, at_value:at_gain],
        sums[3],
        gains[1],
        sums[1],
        sums[2],
        sums[0],
    )


def solution(mesh):
    in_specs = (
        P("fsdp", "ctx", None),
        P("fsdp", None),
        P("fsdp"),
        P("fsdp", None),
        P("fsdp", None),
        P("fsdp", None),
        P("fsdp", None),
        P("fsdp"),
        P("fsdp", None),
        P("fsdp", None),
        P("fsdp", None),
        P("fsdp", "ctx", None),
    )
    out_specs = (
        P("fsdp", "ctx", None),
        P("fsdp", "ctx", None),
        P("fsdp"),
        P("fsdp", None),
        P("fsdp", None),
        P("fsdp", None),
        P("fsdp", None),
        P("fsdp"),
        P("fsdp", None),
        P("fsdp", None),
        P("fsdp", None),
    )
    return jax.shard_map(
        on_device, mesh=mesh, in_specs=in_specs, out_specs=out_specs, check_vma=False
    )
```

time: 1260 us -> 836 us (0.66)
  matrix products: 316 us -> 83.4 us
  waiting for transfers between devices: 637 us -> 482 us
  Pallas kernels: 0 us -> 96.2 us
  local copies, waits for them, and re-layouts: 112 us -> 50.4 us
  other arithmetic: 68.6 us -> 38 us
  blocking collectives: 86.2 us -> 58.6 us
    all_gather x12 -> x4, waiting for transfers between devices: 431 us -> 110 us  [gather_weight(): mine = lax.all_gather(half_of(shard, which), 'fsdp', axis=0, tiled=True)]
    dot_general x28 -> x0, matrix products: 213 us -> none  [the longest x8 71.3 us: block_scores(): jnp.einsum('rgah,kgh->gark', query, key_block, preferred_element_type=jnp...]
    reduce_scatter x2 -> x5, waiting for transfers between devices: 54.3 us -> 175 us  [the longest x3 101 us: scatter_share(): return lax.psum_scatter(mine, 'fsdp', scatter_dimension=0, tiled=True)]
    pallas_call x0 -> x2, Pallas kernels: none -> 96.2 us  [the longest x1 50.7 us: attend_forward(): pl.pallas_call(forward_kernel, grid=(seqs,), in_specs=[whole_block(array)...]
    all_to_all x3 -> x0, waiting for transfers between devices: 65 us -> none  [the longest x1 32.3 us: on_device(): lax.all_to_all(activated, 'fsdp', split_axis=1, concat_axis=0, tiled=True)]
    reduce_sum x4 -> x0, other arithmetic: 35.9 us -> none  [gather_stats(): jnp.sum(terms, axis=3)]
    unnamed x17 -> x16, waiting for transfers between devices: 5.36 us -> 38 us
    all_gather x1, waiting for transfers between devices: 10.5 us -> 38.6 us  [on_device(): lax.all_gather(own_keys, 'ctx', axis=1, tiled=True)]
  transfers between devices with their start and end apart: 20 -> 29, of which waited for: 15 -> 15; matrix products, arithmetic and copies ran while one was open for 21% -> 14% of each run, Pallas kernels for 0% -> 6%
where the time goes in v1:
time: 836 us; the launch traced here: 827 us
  waiting for transfers between devices  482 us (58%)
  Pallas kernels  96.2 us (12%)
  matrix products  83.4 us (10%)
  blocking collectives  58.6 us (7%)
  local copies, waits for them, and re-layouts  50.4 us (6%)
  other arithmetic  38 us (5%)
  between operations  15.1 us (2%)
    all_gather x4, waiting for transfers between devices, gather_weight(): mine = lax.all_gather(half_of(shard, which), 'fsdp', axis=0, tiled=True)  110 us
    reduce_scatter x3, waiting for transfers between devices, scatter_share(): return lax.psum_scatter(mine, 'fsdp', scatter_dimension=0, tiled=True)  101 us
    psum x1, waiting for transfers between devices, sum_share(): mine = lax.psum(part, 'ctx', axis_index_groups=groups)  93.4 us
    pallas_call x1, Pallas kernels, attend_forward(): pl.pallas_call(forward_kernel, grid=(seqs,), in_specs=[whole_block(array)...  50.7 us
    pallas_call x1, Pallas kernels, attend_backward(): pl.pallas_call(backward_kernel, grid=(seqs,), in_specs=[whole_block(array...  45.6 us
    psum x1, blocking collectives, on_device(): gains = lax.psum(jnp.stack([grad_gain_one, grad_gain_two]), ('fsdp', 'ctx'))  39.3 us
    all_gather x1, waiting for transfers between devices, on_device(): lax.all_gather(own_keys, 'ctx', axis=1, tiled=True)  38.6 us
    reduce_scatter x1, waiting for transfers between devices, on_device(): lax.psum_scatter(grad_keys, 'ctx', scatter_dimension=1, tiled=True)  38.5 us
  transfers between devices with their start and end apart: 29, of which 15 were waited for; matrix products, arithmetic and copies ran while one was open for 14% of the time, Pallas kernels for 6%

profile of v1, /device:TPU:0, one launch (start us, length us, event | category | flops | bytes accessed | tf_op | source)
XLA Modules:
  0.0 826.7 jit_solution(12224948261263657425)
XLA Ops:
  11.0 1.3 concatenate.69
  15.6 1.9 constant_dynamic-slice_fusion.2
  17.6 30.6 %all-gather.7.cloned.1.call-done = bf16[960,896]{1,0:T(8,128)(2,1)} async-done(((bf16[240,896]{1,0:T(8,128)(2,1)}), bf16[960,896]{1,0:T(8,128)(2,1)}) %all-gather.7.cloned.1.call-update) | async-done | bytes 1720336 | tf_op jit(solution)/shard_map/all_gather | solution.py:230
  48.9 3.6 copy.92
  52.5 3.6 copy.91
  56.2 3.8 broadcast_select_fusion.6
  63.8 19.3 %all_gather.24 = bf16[960,480]{1,0:T(8,128)(2,1)} all-gather(bf16[240,480]{1,0:T(8,128)(2,1)S(1)} %constant_dynamic-slice_fusion.4), channel_id=1, replica_groups=mesh['fsdp'=4,'ctx'=8] {'fsdp'}, dimensions={0}, use_global_device_ids=true | all-gather | bytes 1152000 | tf_op jit(solution)/shard_map/all_gather | solution.py:230
  83.2 9.1 %all-gather.17.cloned.1.call-done = bf16[2560,480]{0,1:T(8,128)(2,1)} async-done(((bf16[640,480]{0,1:T(8,128)(2,1)}), bf16[2560,480]{0,1:T(8,128)(2,1)}) %all-gather.17.cloned.1.call-update) | async-done | bytes 2457616 | tf_op jit(solution)/shard_map/all_gather | solution.py:230
  92.7 1.6 fusion.45
  95.8 2.0 copy.98.place_ref
  97.8 1.3 copy.120
  99.1 34.0 %all-gather.13.cloned.1.call-done = bf16[960,1280]{1,0:T(8,128)(2,1)} async-done(((bf16[240,1280]{1,0:T(8,128)(2,1)}), bf16[960,1280]{1,0:T(8,128)(2,1)}) %all-gather.13.cloned.1.call-update) | async-done | bytes 2457616 | tf_op jit(solution)/shard_map/all_gather | solution.py:230
  134.3 3.1 broadcast_select_fusion.9
  137.4 36.3 %all-gather.15.cloned.1.call-done = bf16[960,1280]{1,0:T(8,128)(2,1)} async-done(((bf16[240,1280]{1,0:T(8,128)(2,1)}), bf16[960,1280]{1,0:T(8,128)(2,1)}) %all-gather.15.cloned.1.call-update) | async-done | bytes 2457616 | tf_op jit(solution)/shard_map/all_gather | solution.py:230
  173.6 4.9 fusion.14.raw_ref
  178.5 2.0 broadcast_select_fusion.1
  180.6 4.8 fusion.5
  185.3 4.4 broadcast_select_fusion.5
  189.8 2.5 broadcast_select_fusion.3
  192.3 21.1 %all-gather.11.cloned.1.call-done.value_ref = bf16[2,2048,320]{2,1,0:T(8,128)(2,1)} async-done(((bf16[2,256,320]{2,1,0:T(8,128)(2,1)}), bf16[2,2048,320]{2,1,0:T(8,128)(2,1)}) %all-gather.11.cloned.1.call-update) | async-done | bytes 2621456 | tf_op jit(solution)/shard_map/all_gather | solution.py:305
  213.4 38.6 %all-gather.9.cloned.1.call-done.key_ref = bf16[2,2048,320]{2,1,0:T(8,128)(2,1)} async-done(((bf16[2,256,320]{2,1,0:T(8,128)(2,1)}), bf16[2,2048,320]{2,1,0:T(8,128)(2,1)}) %all-gather.9.cloned.1.call-update) | async-done | bytes 2621456 | tf_op jit(solution)/shard_map/all_gather | solution.py:304
  252.1 1.6 copy-done.6
  253.7 50.7 %shard_map.203 = (bf16[2,256,960]{2,1,0:T(8,128)(2,1)S(1)}, bf16[2,256,960]{2,1,0:T(8,128)(2,1)S(1)}, f32[2,15,256]{2,1,0:T(8,128)S(1)}) custom-call(f32[2,256,960]{2,1,0:T(8,128)S(1)} %copy-done.6, bf16[2,2048,320]{2,1,0:T(8,128)(2,1)} %all-gather.9.cloned.1.call-done.key_ref, bf16[2,2048,320]{2,1,0:T(8,128)(2,1)} %all-gather.11.cloned.1.call-done.value_ref, ...), custom_call_target="tpu_custom_call" | custom-call | flops 8053063680 | bytes 5898240 | tf_op jit(solution)/shard_map/pallas_call | solution.py:171
  304.4 1.7 multiply_reduce_fusion.4
  306.8 2.3 copy-done.23
  309.1 4.8 fusion.10
  313.9 10.2 %fusion.2 = (bf16[512,2560]{1,0:T(8,128)(2,1)}, bf16[512,2560]{1,0:T(8,128)(2,1)}, bf16[512,2560]{1,0:T(8,128)(2,1)}) fusion(f32[2560,512]{0,1:T(8,128)} %fusion.5, f32[512,2560]{1,0:T(8,128)} %fusion.10, bf16[512,960]{0,1:T(8,128)(2,1)S(1)} %multiply_convert_fusion.1, bf16[960,1280]{1,0:T(8,128)(2,1)S(1)} %copy-done.26, bf16[960,1280]{1,0:T(8,128)(2,1)S(1)} %copy-done.25), kind=kOutput, calls=%fused_computation.4 | convolution fusion | flops 2547384320 | bytes 24248320 | tf_op jit(solution)/shard_map/dot_general | solution.py:21
  324.1 5.9 fusion.7
  330.0 2.9 convolution_convert_fusion.1
  333.1 3.7 multiply_reduce_fusion
  336.8 2.9 convolution_convert_fusion.2
  340.0 2.9 convolution_convert_fusion
  344.8 2.1 convolution_convert_fusion.4
  347.0 2.3 collective-permute-done.8
  349.3 1.7 add_convert_fusion.5
  351.0 5.3 add_convert_fusion
  356.3 5.3 add_convert_fusion.1
  361.6 5.4 add_convert_fusion.2
  366.9 4.4 copy.115
  372.5 1.3 copy.101
  373.8 45.6 %shard_map.204 = (bf16[2,256,960]{2,1,0:T(8,128)(2,1)}, bf16[2,2048,320]{2,1,0:T(8,128)(2,1)}, bf16[2,2048,320]{2,1,0:T(8,128)(2,1)}) custom-call(bf16[2,256,960]{2,1,0:T(8,128)(2,1)} %copy-done.7, bf16[2,256,960]{2,1,0:T(8,128)(2,1)} %bitcast.113, bf16[2,256,960]{2,1,0:T(8,128)(2,1)} %copy-done.5, ...), custom_call_target="tpu_custom_call" | custom-call | flops 20132659200 | bytes 5898240 | tf_op jit(solution)/shard_map/pallas_call | solution.py:198
  419.4 2.2 copy.116
  422.4 38.5 %reduce-scatter.12.cloned.1.call-done = bf16[2,256,320]{2,1,0:T(8,128)(2,1)} async-done(((bf16[2,2048,320]{2,1,0:T(8,128)(2,1)}), bf16[2,256,320]{2,1,0:T(8,128)(2,1)}) %reduce-scatter.12.cloned.1.call-update) | async-done | bytes 327696 | tf_op jit(solution)/shard_map/reduce_scatter | solution.py:348
  466.6 36.0 %reduce-scatter.14.cloned.1.call-done = bf16[2,256,320]{2,1,0:T(8,128)(2,1)} async-done(((bf16[2,2048,320]{2,1,0:T(8,128)(2,1)}), bf16[2,256,320]{2,1,0:T(8,128)(2,1)}) %reduce-scatter.14.cloned.1.call-update) | async-done | bytes 327696 | tf_op jit(solution)/shard_map/reduce_scatter | solution.py:354
  502.7 3.8 concatenate.84
  506.5 2.8 convolution_convert_fusion.3
  509.4 3.6 collective-permute-done.9
  513.0 2.4 add_convert_fusion.3
  515.5 17.0 %reduce-scatter.16.cloned.1.call-done = bf16[240,480]{1,0:T(8,128)(2,1)} async-done(((bf16[960,480]{1,0:T(8,128)(2,1)}), bf16[240,480]{1,0:T(8,128)(2,1)}) %reduce-scatter.16.cloned.1.call-update) | async-done | bytes 230416 | tf_op jit(solution)/shard_map/reduce_scatter | solution.py:242
  532.5 41.9 %reduce-scatter.18.cloned.1.call-done = bf16[240,1280]{1,0:T(8,128)(2,1)} async-done(((bf16[960,1280]{1,0:T(8,128)(2,1)}), bf16[240,1280]{1,0:T(8,128)(2,1)}) %reduce-scatter.18.cloned.1.call-update) | async-done | bytes 614416 | tf_op jit(solution)/shard_map/reduce_scatter | solution.py:242
  574.3 41.7 %reduce-scatter.20.cloned.1.call-done = bf16[240,1280]{1,0:T(8,128)(2,1)} async-done(((bf16[960,1280]{1,0:T(8,128)(2,1)}), bf16[240,1280]{1,0:T(8,128)(2,1)}) %reduce-scatter.20.cloned.1.call-update) | async-done | bytes 614416 | tf_op jit(solution)/shard_map/reduce_scatter | solution.py:242
  616.1 35.9 %reduce-scatter.24.cloned.1.call-done = bf16[240,896]{1,0:T(8,128)(2,1)} async-done(((bf16[960,896]{1,0:T(8,128)(2,1)}), bf16[240,896]{1,0:T(8,128)(2,1)}) %reduce-scatter.24.cloned.1.call-update) | async-done | bytes 430096
  652.0 6.6 add_convert_fusion.6
  659.7 1.2 fusion.57
  661.9 2.4 multiply_reduce_fusion.1
  664.3 93.4 %all-reduce.4.cloned.1.call-done = (bf16[240,896]{1,0:T(8,128)(2,1)}, bf16[240,480]{1,0:T(8,128)(2,1)}, bf16[240,1280]{1,0:T(8,128)(2,1)}, bf16[240,1280]{1,0:T(8,128)(2,1)}, bf16[640,480]{0,1:T(8,128)(2,1)}) async-done(((bf16[240,896]{1,0:T(8,128)(2,1)}, bf16[240,480]{1,0:T(8,128)(2,1)}, bf16[240,1280]{1,0:T(8,128)(2,1)}, bf16[240,1280]{1,0:T(8,128)(2,1)}, bf16[640,480]{0,1:T(8,128)(2,1)}), ...) | async-done | bytes 2503696 | tf_op jit(solution)/shard_map/psum | solution.py:248
  757.8 4.7 add_convert_fusion.4
  762.4 39.3 %psum.42 = f32[2,960]{1,0:T(2,128)S(1)} all-reduce(f32[2,960]{1,0:T(2,128)S(1)} %pad_maximum_fusion.21), channel_id=1, replica_groups=mesh['fsdp'=4,'ctx'=8] {'fsdp','ctx'}, use_global_device_ids=true, to_apply=%region_9.10 | all-reduce | flops 1920 | bytes 15360 | tf_op jit(solution)/shard_map/psum | solution.py:391
  802.4 2.2 copy.125
  811.0 1.3 broadcast_select_fusion.13
  813.6 1.6 maximum_convert_fusion.2
  815.2 1.7 maximum_convert_fusion.1
  817.0 1.3 broadcast_select_fusion.15
  818.2 1.7 maximum_convert_fusion
  (230 shorter events, 35.7 us)
Async XLA Ops:
  7.2 6.1 copy-start
  7.2 41.0 %all-gather.7.cloned.1.call-start = ((), (), s32[]{:S(2)}) async-start(), calls=%async_computation.7 | async-start | bytes 2150400 | tf_op jit(solution)/shard_map/all_gather | solution.py:230
  13.2 79.1 %all-gather.17.cloned.1.call-start = ((), (), s32[]{:S(2)}) async-start(), calls=%async_computation.12 | async-start | bytes 3072000 | tf_op jit(solution)/shard_map/all_gather | solution.py:230
  14.1 34.1 %copy-start.17 = (bf16[2,256,960]{1,2,0:T(8,128)(2,1)S(1)}, bf16[2,256,960]{1,2,0:T(8,128)(2,1)}, u32[]{:S(2)}) copy-start(bf16[2,256,960]{1,2,0:T(8,128)(2,1)} %param.12) | copy-start | bytes 2949124
  14.2 118.9 %all-gather.13.cloned.1.call-start = ((), (), s32[]{:S(2)}) async-start(), calls=%async_computation.10 | async-start | bytes 3072000 | tf_op jit(solution)/shard_map/all_gather | solution.py:230
  15.5 158.1 %all-gather.15.cloned.1.call-start = ((), (), s32[]{:S(2)}) async-start(), calls=%async_computation.11 | async-start | bytes 3072000 | tf_op jit(solution)/shard_map/all_gather | solution.py:230
  17.6 195.8 %all-gather.11.cloned.1.call-start = ((), (), s32[]{:S(2)}) async-start(), calls=%async_computation.9 | async-start | bytes 3538944 | tf_op jit(solution)/shard_map/all_gather | solution.py:305
  48.2 4.3 collective-permute-start
  61.2 31.5 %copy-start.31 = (bf16[512,960]{0,1:T(8,128)(2,1)}, bf16[512,960]{0,1:T(8,128)(2,1)S(1)}, u32[]{:S(2)}) copy-start(bf16[512,960]{0,1:T(8,128)(2,1)S(1)} %multiply_convert_fusion.2) | copy-start | bytes 2949124
  61.2 21.9 %copy-start.42 = (s32[2,2048]{1,0:T(2,128)S(1)}, s32[2,2048]{1,0:T(2,128)}, u32[]{:S(2)}) copy-start(s32[2,2048]{1,0:T(2,128)} %param.13) | copy-start | bytes 49156
  62.7 189.4 %all-gather.9.cloned.1.call-start = ((), (), s32[]{:S(2)}) async-start(), calls=%async_computation.8 | async-start | bytes 3538944 | tf_op jit(solution)/shard_map/all_gather | solution.py:304
  83.1 51.2 %collective-permute-start.1 = (bf16[960,480]{1,0:T(8,128)(2,1)}, bf16[960,480]{1,0:T(8,128)(2,1)}, u32[]{:S(2)}, u32[]{:S(2)}) collective-permute-start(bf16[960,480]{1,0:T(8,128)(2,1)} %all_gather.24), channel_id=1, source_target_pairs={{0,1},{1,0},{2,3},{3,2},{4,5},{5,4},{6,7},{7,6},{8,9},{9,8},{10,11... | collective-permute-start | bytes 2764808 | tf_op jit(solution)/shard_map/ppermute | solution.py:219
  83.2 11.4 %copy-start.45 = (f32[1,2,2,128]{3,1,2,0:T(2,128)}, f32[1,2,2,128]{3,1,2,0:T(2,128)S(1)}, u32[]{:S(2)}) copy-start(f32[1,2,2,128]{3,1,2,0:T(2,128)S(1)} %copy.122) | copy-start | bytes 6148
  83.2 49.9 %copy-start.49 = (f32[32]{0:T(128)}, f32[32]{0:T(128)S(1)}, u32[]{:S(2)}) copy-start(f32[32]{0:T(128)S(1)} %multiply_exponential_fusion) | copy-start | bytes 388
  83.2 11.3 %copy-start.52 = (pred[320]{0:T(512)(128)(4,1)}, pred[320]{0:T(512)(128)(4,1)S(1)}, u32[]{:S(2)}) copy-start(pred[320]{0:T(512)(128)(4,1)S(1)} %and_compare_fusion) | copy-start | bytes 964
  92.3 86.2 %collective-permute-start.4 = (bf16[2560,480]{0,1:T(8,128)(2,1)}, bf16[2560,480]{0,1:T(8,128)(2,1)}, u32[]{:S(2)}, u32[]{:S(2)}) collective-permute-start(bf16[2560,480]{0,1:T(8,128)(2,1)} %all-gather.17.cloned.1.call-done), channel_id=1, source_target_pairs={{0,1},{1,0},{2,3},{3,2},{4,5},{5,4},{6,7},{7,6},{8,9},{9,8},{10,11... | collective-permute-start | bytes 7372808 | tf_op jit(solution)/shard_map/ppermute | solution.py:219
  95.7 323.7 %reduce-scatter.22.cloned.1.call-start = ((), (), s32[]{:S(2)}) async-start(), calls=%async_computation.18 | async-start | bytes 3276800
  95.8 156.2 %copy-start.4 = (s32[2,1,256]{2,1,0:T(1,128)}, s32[2,1,256]{2,1,0:T(1,128)S(1)}, u32[]{:S(2)}) copy-start(s32[2,1,256]{2,1,0:T(1,128)S(1)} %broadcast_in_dim.15.own_ref) | copy-start | bytes 6148
  99.1 262.5 %copy-start.12 = (bf16[2,120,8,256]{3,2,0,1:T(8,128)(2,1)}, bf16[2,120,8,256]{3,2,0,1:T(8,128)(2,1)S(1)}, u32[]{:S(2)}) copy-start(bf16[2,120,8,256]{3,2,0,1:T(8,128)(2,1)S(1)} %copy.120) | copy-start | bytes 2949124
  133.1 52.3 %collective-permute-start.2 = (bf16[960,1280]{1,0:T(8,128)(2,1)}, bf16[960,1280]{1,0:T(8,128)(2,1)}, u32[]{:S(2)}, u32[]{:S(2)}) collective-permute-start(bf16[960,1280]{1,0:T(8,128)(2,1)} %all-gather.13.cloned.1.call-done), channel_id=1, source_target_pairs={{0,1},{1,0},{2,3},{3,2},{4,5},{5,4},{6,7},{7,6},{8,9},{9,8},{10,11... | collective-permute-start | bytes 7372808 | tf_op jit(solution)/shard_map/ppermute | solution.py:219
  134.3 117.8 %copy-start.2 = (f32[2,256,64]{2,1,0:T(8,128)}, f32[2,256,64]{2,1,0:T(8,128)S(1)}, u32[]{:S(2)}) copy-start(f32[2,256,64]{2,1,0:T(8,128)S(1)} %get-tuple-element.155.cos_ref) | copy-start | bytes 393220
  134.3 117.8 %copy-start.3 = (f32[2,256,64]{2,1,0:T(8,128)}, f32[2,256,64]{2,1,0:T(8,128)S(1)}, u32[]{:S(2)}) copy-start(f32[2,256,64]{2,1,0:T(8,128)S(1)} %get-tuple-element.156.sin_ref) | copy-start | bytes 393220
  173.6 16.1 %collective-permute-start.3 = (bf16[960,1280]{1,0:T(8,128)(2,1)}, bf16[960,1280]{1,0:T(8,128)(2,1)S(1)}, u32[]{:S(2)}, u32[]{:S(2)}) collective-permute-start(bf16[960,1280]{1,0:T(8,128)(2,1)} %all-gather.15.cloned.1.call-done), channel_id=1, source_target_pairs={{0,1},{1,0},{2,3},{3,2},{4,5},{5,4},{6,7},{7,6},{8,9},{9,8},{10,11... | collective-permute-start | bytes 7372808 | tf_op jit(solution)/shard_map/ppermute | solution.py:219
  173.6 4.9 copy-start.20
  180.5 4.8 copy-start.18
  180.5 4.8 copy-start.19
  180.5 4.8 copy-start.21
  253.7 50.7 %copy-start.35 = (bf16[960,480]{1,0:T(8,128)(2,1)S(1)}, bf16[960,480]{1,0:T(8,128)(2,1)}, u32[]{:S(2)}) copy-start(bf16[960,480]{1,0:T(8,128)(2,1)} %get-tuple-element.111) | copy-start | bytes 2764804
  253.7 50.7 %copy-start.36 = (bf16[960,480]{1,0:T(8,128)(2,1)S(1)}, bf16[960,480]{1,0:T(8,128)(2,1)}, u32[]{:S(2)}) copy-start(bf16[960,480]{1,0:T(8,128)(2,1)} %get-tuple-element.112) | copy-start | bytes 2764804
  304.4 44.9 %copy-start.5 = (bf16[2,256,960]{2,1,0:T(8,128)(2,1)}, bf16[2,256,960]{2,1,0:T(8,128)(2,1)S(1)}, u32[]{:S(2)}) copy-start(bf16[2,256,960]{2,1,0:T(8,128)(2,1)S(1)} %get-tuple-element.28.out_ref) | copy-start | bytes 2949124
  306.2 36.9 %copy-start.9 = (f32[512,960]{0,1:T(8,128)}, f32[512,960]{0,1:T(8,128)S(1)}, u32[]{:S(2)}) copy-start(f32[512,960]{0,1:T(8,128)S(1)} %get-tuple-element.150) | copy-start | bytes 5898244
  306.2 36.9 %copy-start.43 = (f32[512]{0:T(512)}, f32[512]{0:T(512)S(1)}, u32[]{:S(2)}) copy-start(f32[512]{0:T(512)S(1)} %get-tuple-element.145) | copy-start | bytes 6148
  306.5 30.3 %copy-start.33 = (bf16[512,960]{0,1:T(8,128)(2,1)}, bf16[512,960]{0,1:T(8,128)(2,1)S(1)}, u32[]{:S(2)}) copy-start(bf16[512,960]{0,1:T(8,128)(2,1)S(1)} %multiply_convert_fusion.1) | copy-start | bytes 2949124
  309.1 4.8 copy-start.25
  309.1 4.8 copy-start.26
  324.1 5.9 copy-start.55
  332.8 18.2 %collective-permute-start.7 = (bf16[960,1280]{1,0:T(8,128)(2,1)}, bf16[960,1280]{1,0:T(8,128)(2,1)}, u32[]{:S(2)}, u32[]{:S(2)}) collective-permute-start(bf16[960,1280]{1,0:T(8,128)(2,1)} %convolution_convert_fusion.1), channel_id=1, source_target_pairs={{0,1},{1,0},{2,3},{3,2},{4,5},{5,4},{6,7},{7,6},{8,9},{9,8},{10,11... | collective-permute-start | bytes 7372808 | tf_op jit(solution)/shard_map/ppermute | solution.py:219
  336.8 6.3 copy-start.14
  339.7 16.6 %collective-permute-start.6 = (bf16[960,1280]{1,0:T(8,128)(2,1)}, bf16[960,1280]{1,0:T(8,128)(2,1)}, u32[]{:S(2)}, u32[]{:S(2)}) collective-permute-start(bf16[960,1280]{1,0:T(8,128)(2,1)} %convolution_convert_fusion.2), channel_id=1, source_target_pairs={{0,1},{1,0},{2,3},{3,2},{4,5},{5,4},{6,7},{7,6},{8,9},{9,8},{10,11... | collective-permute-start | bytes 7372808 | tf_op jit(solution)/shard_map/ppermute | solution.py:219
  342.9 18.7 %collective-permute-start.5 = (bf16[2560,480]{0,1:T(8,128)(2,1)}, bf16[2560,480]{0,1:T(8,128)(2,1)}, u32[]{:S(2)}, u32[]{:S(2)}) collective-permute-start(bf16[2560,480]{0,1:T(8,128)(2,1)} %convolution_convert_fusion), channel_id=1, source_target_pairs={{0,1},{1,0},{2,3},{3,2},{4,5},{5,4},{6,7},{7,6},{8,9},{9,8},{10,11... | collective-permute-start | bytes 7372808 | tf_op jit(solution)/shard_map/ppermute | solution.py:219
  344.5 4.8 collective-permute-start.8
  371.4 89.6 %reduce-scatter.12.cloned.1.call-start = ((), (), s32[]{:S(2)}) async-start(), calls=%async_computation.13 | async-start | bytes 3538944 | tf_op jit(solution)/shard_map/reduce_scatter | solution.py:348
  421.6 81.0 %reduce-scatter.14.cloned.1.call-start = ((), (), s32[]{:S(2)}) async-start(), calls=%async_computation.14 | async-start | bytes 3538944 | tf_op jit(solution)/shard_map/reduce_scatter | solution.py:354
  422.4 110.1 %reduce-scatter.16.cloned.1.call-start = ((), (), s32[]{:S(2)}) async-start(), calls=%async_computation.15 | async-start | bytes 1228800 | tf_op jit(solution)/shard_map/reduce_scatter | solution.py:242
  462.0 112.3 %reduce-scatter.18.cloned.1.call-start = ((), (), s32[]{:S(2)}) async-start(), calls=%async_computation.16 | async-start | bytes 3072000 | tf_op jit(solution)/shard_map/reduce_scatter | solution.py:242
  462.7 153.3 %reduce-scatter.20.cloned.1.call-start = ((), (), s32[]{:S(2)}) async-start(), calls=%async_computation.17 | async-start | bytes 3072000 | tf_op jit(solution)/shard_map/reduce_scatter | solution.py:242
  463.3 188.6 %reduce-scatter.24.cloned.1.call-start = ((), (), s32[]{:S(2)}) async-start(), calls=%async_computation.19 | async-start | bytes 2150400
  506.5 6.5 copy-start.27
  506.5 6.5 copy-start.32
  509.3 3.7 collective-permute-start.9
  515.4 242.3 %all-reduce.4.cloned.1.call-start = ((), (), s32[]{:S(2)}) async-start(), calls=%async_computation.20 | async-start | bytes 5038080 | tf_op jit(solution)/shard_map/psum | solution.py:248
  652.0 7.7 copy-start.11
  652.0 7.7 copy-start.15
  652.0 7.7 copy-start.16
  661.9 95.8 %copy-start.13 = (bf16[2,120,8,256]{3,2,0,1:T(8,128)(2,1)S(1)}, bf16[2,120,8,256]{3,2,0,1:T(8,128)(2,1)}, u32[]{:S(2)}) copy-start(bf16[2,120,8,256]{3,2,0,1:T(8,128)(2,1)} %copy-done.12) | copy-start | bytes 2949124
  661.9 95.8 %copy-start.44 = (f32[512]{0:T(512)S(1)}, f32[512]{0:T(512)}, u32[]{:S(2)}) copy-start(f32[512]{0:T(512)} %copy-done.43) | copy-start | bytes 6148
  661.9 95.8 %copy-start.48 = (f32[512]{0:T(512)S(1)}, f32[512]{0:T(512)}, u32[]{:S(2)}) copy-start(f32[512]{0:T(512)} %copy-done.47) | copy-start | bytes 6148
  757.7 47.9 %collective-permute-start.11 = (bf16[240,480]{1,0:T(8,128)(2,1)}, bf16[240,480]{1,0:T(8,128)(2,1)}, u32[]{:S(2)}, u32[]{:S(2)}) collective-permute-start(bf16[240,480]{1,0:T(8,128)(2,1)} %get-tuple-element.94), channel_id=1, source_target_pairs={{0,1},{1,0},{2,3},{3,2},{4,5},{5,4},{6,7},{7,6},{8,9},{9,8},{10,11... | collective-permute-start | bytes 691208 | tf_op jit(solution)/shard_map/ppermute | solution.py:219
  757.7 4.7 copy-start.51
  757.7 44.0 %copy-start.40 = (bf16[240,896]{1,0:T(8,128)(2,1)S(1)}, bf16[240,896]{1,0:T(8,128)(2,1)}, u32[]{:S(2)}) copy-start(bf16[240,896]{1,0:T(8,128)(2,1)} %get-tuple-element.93) | copy-start | bytes 1290244
  801.8 6.1 collective-permute-start.10
  804.6 7.8 collective-permute-start.14
  805.1 5.9 collective-permute-start.13
  805.1 11.8 %collective-permute-start.12 = (bf16[240,1280]{1,0:T(8,128)(2,1)}, bf16[240,1280]{1,0:T(8,128)(2,1)}, u32[]{:S(2)}, u32[]{:S(2)}) collective-permute-start(bf16[240,1280]{1,0:T(8,128)(2,1)} %get-tuple-element.95), channel_id=1, source_target_pairs={{0,1},{1,0},{2,3},{3,2},{4,5},{5,4},{6,7},{7,6},{8,9},{9,8},{10,11... | collective-permute-start | bytes 1843208 | tf_op jit(solution)/shard_map/ppermute | solution.py:219
  (22 other events, 45.0 us)
Sparse Core Ops, SparseCore 0:
  13.3 34.8 all-gather.6
  50.6 41.6 all-gather.16
  94.7 38.2 all-gather.12
  135.3 38.2 all-gather.14
  175.1 38.2 all-gather.10
  214.9 37.1 all-gather.8
  371.5 38.4 reduce-scatter.21
  421.7 39.1 reduce-scatter.11
  463.2 39.4 reduce-scatter.13
  506.0 26.3 reduce-scatter.15
  536.1 38.1 reduce-scatter.17
  577.8 38.1 reduce-scatter.19
  619.7 32.2 reduce-scatter.23
  655.4 102.3 all-reduce.3
